TPU v7x, 32 devices: a whole 2x2x4 slice. The times are simulated.
32 devices in a mesh: row: 2 (over x), col: 4 (over z), rep: 4 (over y, core).
Axes of the slice: x: 2, y: 2, z: 4, core: 2. Of those that a mesh axis runs over, the one named last changes fastest.
Arguments:
- features: bfloat16 [2048, 512], P(('col', 'row'), 'rep'), may hold values from -6 to 6
- weight: bfloat16 [512, 512], replicated, may hold values from -0.25 to 0.25
- tile_pos: int32 [2, 4, 32], P('row', 'col'), may hold values from 0 to 31
- edges: int32 [2, 4, 32, 64], P('row', 'col'), may hold values from -1 to 16383, as said below
- degree: int32 [2048], P(('row', 'col')), may hold values from 16 to 96
- cotangent: bfloat16 [2048, 512], P(('row', 'col'), 'rep'), may hold values from -6 to 6
Outputs:
- output: bfloat16 [2048, 512], P(('row', 'col'), 'rep')
- grad_weight: float32 [512, 512], P('rep')
- grad_features: bfloat16 [2048, 512], P(('col', 'row'), 'rep')
Inputs may be any that keep to these rules, and one draw needn't show every extreme that they name: -1 marks an empty slot, any other value is 128 times the target's place in the tile plus the source's place. In each block the live tiles come first and an empty tile holds only -1; within a tile the live slots come first; some block has all 32 tiles live, and every live tile holds 1 to 64 edges.
All inputs are finite; a program needn't handle non-finite values.
Results may differ from a plain program's by a relative error of at most 0.0058.
Values may be sent and summed in bfloat16 or wider, within the bound.
A program may use at most 64 MiB of HBM per device.

v0:
```python
import math

import jax
import jax.numpy as jnp
from jax import lax
from jax.sharding import PartitionSpec as P


def build_tiles(slot_rows):
    live_mask = slot_rows >= 0
    targets = jnp.where(live_mask, slot_rows // 128, -1)
    sources = jnp.where(live_mask, slot_rows % 128, -1)
    lane_ids = jnp.arange(128, dtype=jnp.int32)
    target_hot = (targets[:, :, None] == lane_ids).astype(jnp.bfloat16)
    source_hot = (sources[:, :, None] == lane_ids).astype(jnp.bfloat16)
    tiles = jnp.einsum("gea,geb->gab", target_hot, source_hot, preferred_element_type=jnp.float32)
    return tiles.astype(jnp.bfloat16)


def aggregate_range(places, slots, source_rows, first_row, row_count, col_tiles, transpose):
    tile_count = places.shape[0]
    group_size = math.gcd(tile_count, 32)
    feature_width = source_rows.shape[1]
    blocks = source_rows.reshape(-1, 128, feature_width)
    place_groups = places.reshape(tile_count // group_size, group_size)
    slot_groups = slots.reshape(tile_count // group_size, group_size, slots.shape[1])
    lane_ids = jnp.arange(128, dtype=jnp.int32)

    def step(totals, item):
        place_row, slot_rows = item
        tiles = build_tiles(slot_rows)
        row_index = place_row // col_tiles
        col_index = place_row % col_tiles
        if transpose:
            picked = blocks[row_index]
            products = jnp.einsum("gab,gaf->gbf", tiles, picked, preferred_element_type=jnp.float32)
            landing = col_index
        else:
            picked = blocks[col_index]
            products = jnp.einsum("gab,gbf->gaf", tiles, picked, preferred_element_type=jnp.float32)
            landing = row_index
        node_rows = (landing[:, None] * 128 + lane_ids[None, :]).reshape(-1) - first_row
        inside = (node_rows >= 0) & (node_rows < row_count)
        node_rows = jnp.where(inside, node_rows, row_count)
        flat = products.reshape(-1, feature_width)
        return (totals.at[node_rows].add(flat, mode="drop"), None)

    start = jnp.zeros((row_count, feature_width), jnp.float32)
    totals, _ = lax.scan(step, start, (place_groups, slot_groups))
    return totals


def body(features, weight, tile_pos, edges, degree, cotangent):
    sub_rows = features.shape[0]
    row_count = lax.axis_size("row")
    col_count = lax.axis_size("col")
    col_tiles = sub_rows * row_count // 128
    target_total = sub_rows * col_count
    source_total = sub_rows * row_count
    places = tile_pos.reshape(-1)
    slots = edges.reshape(places.shape[0], edges.shape[-1])
    block_rows = lax.all_gather(features, "row", axis=0, tiled=True)
    partial_value = aggregate_range(places, slots, block_rows, 0, target_total, col_tiles, False)
    summed = lax.psum_scatter(partial_value, "col", scatter_dimension=0, tiled=True)
    inverse = 1.0 / degree.astype(jnp.float32)
    agg = (summed * inverse[:, None]).astype(jnp.bfloat16)
    replica = lax.axis_index("rep")
    in_width = agg.shape[1]
    out_width = cotangent.shape[1]
    weight_rows = lax.dynamic_slice_in_dim(weight, replica * in_width, in_width, 0)
    weight_cols = lax.dynamic_slice_in_dim(weight, replica * out_width, out_width, 1)
    agg_full = lax.all_gather(agg, "rep", axis=1, tiled=True)
    preact = jnp.dot(agg_full, weight_cols, preferred_element_type=jnp.float32)
    sigmoid_pre = jax.nn.sigmoid(preact)
    output = (preact * sigmoid_pre).astype(jnp.bfloat16)
    silu_slope = sigmoid_pre * (1.0 + preact * (1.0 - sigmoid_pre))
    grad_pre = (cotangent.astype(jnp.float32) * silu_slope).astype(jnp.bfloat16)
    grad_full = lax.all_gather(grad_pre, "rep", axis=1, tiled=True)
    grad_agg = lax.dot_general(
        grad_full, weight_rows, (((1,), (1,)), ((), ())), preferred_element_type=jnp.float32
    )
    local_weight = lax.dot_general(
        agg, grad_full, (((0,), (0,)), ((), ())), preferred_element_type=jnp.float32
    )
    grad_weight = lax.psum(local_weight, ("row", "col"))
    scaled = (grad_agg * inverse[:, None]).astype(jnp.bfloat16)
    target_rows = lax.all_gather(scaled, "col", axis=0, tiled=True)
    backward_sum = aggregate_range(places, slots, target_rows, 0, source_total, col_tiles, True)
    back_total = lax.psum_scatter(backward_sum, "row", scatter_dimension=0, tiled=True)
    grad_features = back_total.astype(jnp.bfloat16)
    return (output, grad_weight, grad_features)


def solution(mesh):
    placed = (
        P(("col", "row"), "rep"),
        P(),
        P("row", "col", None),
        P("row", "col", None, None),
        P(("row", "col")),
        P(("row", "col"), "rep"),
    )
    return jax.shard_map(
        body,
        mesh=mesh,
        in_specs=placed,
        out_specs=(P(("row", "col"), "rep"), P("rep", None), P(("col", "row"), "rep")),
        check_vma=False,
    )
```

profile of v0, /device:TPU:0, one launch (start us, length us, event | category | flops | bytes accessed | tf_op | source)
XLA Modules:
  0.0 214.0 jit_solution(8652043665613392843)
XLA Ops:
  7.2 0.0 copy-start
  7.2 0.0 reduce-scatter.3.cloned.1.call-start
  7.2 0.7 fusion.17
  7.9 0.7 fusion.15
  8.6 0.1 iota_add_fusion
  8.7 0.7 fusion.10
  9.5 6.1 %all_gather.12 = bf16[512,128]{1,0:T(8,128)(2,1)S(1)} all-gather(bf16[256,128]{1,0:T(8,128)(2,1)} %param.6), channel_id=1, replica_groups=mesh['row'=2,'col'=4,'rep'=4] {'row'}, dimensions={0}, use_global_device_ids=true | all-gather | bytes 196608 | tf_op jit(solution)/shard_map/all_gather | solution.py:62
  15.6 0.7 gather_fusion
  16.3 1.5 convolution_convert_fusion
  17.9 0.0 copy-start.1
  17.9 1.8 fusion.21
  19.7 23.4 %scatter_custom_fusion = f32[1024,128]{1,0:T(8,128)} fusion(s32[4096]{0:T(1024)S(1)} %bitcast.92, f32[4096,128]{1,0:T(8,128)} %bitcast.88, f32[]{:T(128)} %constant.105.clone.1), kind=kCustom, calls=%fused_computation.11 | custom fusion | flops 524288 | bytes 524800 | tf_op jit(solution)/shard_map/while/body/eval_jaxpr/scatter-add | solution.py:46
  43.1 0.0 reduce-scatter.3.cloned.1.call-update
  43.1 0.0 reduce-scatter.5.cloned.1.call-start
  43.2 23.4 %reduce-scatter.3.cloned.1.call-done = f32[256,128]{1,0:T(8,128)} async-done(((f32[1024,128]{1,0:T(8,128)}), f32[256,128]{1,0:T(8,128)}) %reduce-scatter.3.cloned.1.call-update) | async-done | bytes 131088 | tf_op jit(solution)/shard_map/reduce_scatter | solution.py:64
  66.7 1.0 multiply_convert_fusion.2
  67.7 5.8 %all_gather.13 = bf16[256,512]{1,0:T(8,128)(2,1)S(1)} all-gather(bf16[256,128]{1,0:T(8,128)(2,1)S(1)} %multiply_convert_fusion.2), channel_id=1, replica_groups=mesh['row'=2,'col'=4,'rep'=4] {'rep'}, dimensions={1}, use_global_device_ids=true | all-gather | bytes 327680 | tf_op jit(solution)/shard_map/all_gather | solution.py:72
  73.5 0.9 multiply_convert_fusion
  74.3 5.9 %all_gather.14 = bf16[256,512]{1,0:T(8,128)(2,1)S(1)} all-gather(bf16[256,128]{1,0:T(8,128)(2,1)S(1)} %get-tuple-element.27), channel_id=1, replica_groups=mesh['row'=2,'col'=4,'rep'=4] {'rep'}, dimensions={1}, use_global_device_ids=true | all-gather | bytes 327680 | tf_op jit(solution)/shard_map/all_gather | solution.py:78
  80.2 0.2 fusion
  80.5 14.4 %all_gather.15 = bf16[1024,128]{1,0:T(8,128)(2,1)S(1)} all-gather(bf16[256,128]{1,0:T(8,128)(2,1)S(1)} %fusion), channel_id=1, replica_groups=mesh['row'=2,'col'=4,'rep'=4] {'col'}, dimensions={0}, use_global_device_ids=true | all-gather | bytes 327680 | tf_op jit(solution)/shard_map/all_gather | solution.py:87
  94.8 0.7 gather_fusion.1
  95.6 1.9 fusion.23
  97.5 23.3 %scatter_custom_fusion.1 = f32[512,128]{1,0:T(8,128)} fusion(s32[4096]{0:T(1024)S(1)} %bitcast.91, f32[4096,128]{1,0:T(8,128)} %bitcast.87, f32[]{:T(128)} %constant.105.clone.1), kind=kCustom, calls=%fused_computation.14 | custom fusion | flops 524288 | bytes 262656 | tf_op jit(solution)/shard_map/while/body/eval_jaxpr/scatter-add | solution.py:46
  120.8 0.0 reduce-scatter.5.cloned.1.call-update
  120.8 0.0 all-reduce.2.cloned.1.call-start
  120.9 0.9 fusion.22
  121.8 0.0 all-reduce.2.cloned.1.call-update
  121.8 9.0 %reduce-scatter.5.cloned.1.call-done = f32[256,128]{1,0:T(8,128)} async-done(((f32[512,128]{1,0:T(8,128)}), f32[256,128]{1,0:T(8,128)}) %reduce-scatter.5.cloned.1.call-update) | async-done | bytes 131088 | tf_op jit(solution)/shard_map/reduce_scatter | solution.py:89
  130.8 1.5 convert_element_type.42
  132.4 73.4 %all-reduce.2.cloned.1.call-done = f32[128,512]{1,0:T(8,128)} async-done(((f32[128,512]{1,0:T(8,128)}), f32[128,512]{1,0:T(8,128)}) %all-reduce.2.cloned.1.call-update) | async-done | bytes 262160 | tf_op jit(solution)/shard_map/psum | solution.py:85
  205.8 1.7 copy.13
  (9 shorter events, 0.1 us)
Async XLA Ops:
  7.2 66.3 %copy-start = (bf16[512,512]{1,0:T(8,128)(2,1)S(1)}, bf16[512,512]{1,0:T(8,128)(2,1)}, u32[]{:S(2)}) copy-start(bf16[512,512]{1,0:T(8,128)(2,1)} %param.7) | copy-start | bytes 1572868
  7.2 59.5 %reduce-scatter.3.cloned.1.call-start = ((), (), s32[]{:S(2)}) async-start(), calls=%async_computation.2 | async-start | bytes 655360 | tf_op jit(solution)/shard_map/reduce_scatter | solution.py:64
  17.9 25.3 %copy-start.1 = (s32[256]{0:T(256)S(1)}, s32[256]{0:T(256)}, u32[]{:S(2)}) copy-start(s32[256]{0:T(256)} %param.10) | copy-start | bytes 3076
  17.9 55.6 %copy-start.2 = (bf16[256,128]{1,0:T(8,128)(2,1)S(1)}, bf16[256,128]{1,0:T(8,128)(2,1)}, u32[]{:S(2)}) copy-start(bf16[256,128]{1,0:T(8,128)(2,1)} %param.11) | copy-start | bytes 196612
  43.1 87.7 %reduce-scatter.5.cloned.1.call-start = ((), (), s32[]{:S(2)}) async-start(), calls=%async_computation.4 | async-start | bytes 393216 | tf_op jit(solution)/shard_map/reduce_scatter | solution.py:89
  120.8 84.9 %all-reduce.2.cloned.1.call-start = ((), (), s32[]{:S(2)}) async-start(), calls=%async_computation.3 | async-start | bytes 524288 | tf_op jit(solution)/shard_map/psum | solution.py:85
Sparse Core Ops, SparseCore 0:
  43.2 23.3 reduce-scatter.2
  120.9 9.8 reduce-scatter.4
  135.1 70.5 all-reduce.1
where the time goes:
time: 214 us
  waiting for transfers between devices  106 us (50%)
  other arithmetic  51.6 us (24%)
  blocking collectives  32.2 us (15%)
  between operations  13.9 us (6%)
  matrix products  7.16 us (3%)
  local copies, waits for them, and re-layouts  3.19 us (1%)
    psum x1, waiting for transfers between devices, body(): grad_weight = lax.psum(local_weight, ('row', 'col'))  73.4 us
    scatter-add x2, other arithmetic, step(): return (totals.at[node_rows].add(flat, mode='drop'), None)  46.8 us
    reduce_scatter x1, waiting for transfers between devices, body(): lax.psum_scatter(partial_value, 'col', scatter_dimension=0, tiled=True)  23.4 us
    all_gather x1, blocking collectives, body(): target_rows = lax.all_gather(scaled, 'col', axis=0, tiled=True)  14.4 us
    reduce_scatter x1, waiting for transfers between devices, body(): lax.psum_scatter(backward_sum, 'row', scatter_dimension=0, tiled=True)  9 us
    all_gather x1, blocking collectives, body(): block_rows = lax.all_gather(features, 'row', axis=0, tiled=True)  6.11 us
    all_gather x1, blocking collectives, body(): grad_full = lax.all_gather(grad_pre, 'rep', axis=1, tiled=True)  5.9 us
    all_gather x1, blocking collectives, body(): agg_full = lax.all_gather(agg, 'rep', axis=1, tiled=True)  5.81 us
  transfers between devices with their start and end apart: 3, of which 3 were waited for; matrix products, arithmetic and copies ran while one was open for 1% of the time, Pallas kernels for 0%

commit v1 on v0

v1 whole, which is shorter than its diff:
```python
import functools
import math

import jax
import jax.numpy as jnp
from jax import lax
from jax.experimental import pallas as pl
from jax.experimental.pallas import tpu as pltpu
from jax.sharding import PartitionSpec as P

MESH = pl.DeviceIdType.MESH
BF16 = jnp.bfloat16
F32 = jnp.float32
TILE = 128


def repeat(count, step):
    if count <= 16:
        for index in range(count):
            step(index)
    else:
        lax.fori_loop(0, count, lambda index, carry: (step(index), carry)[1], 0)


def start_of(index, size):
    return index * size if isinstance(index, int) else pl.multiple_of(index * size, size)


def one_hot(values, height):
    ids = lax.broadcasted_iota(jnp.int32, (height, values.shape[1]), 0).astype(F32) + 1.0
    return jnp.where(values == ids, 1.0, 0.0).astype(BF16)


def kernel(
    fused,
    feat_ref, weight_hbm, pos_ref, edges_ref, deg_ref, cot_ref,
    out_ref, gw_ref, gf_ref,
    weight_buf, tsort, ssort, adj, adj_t, xbuf, cot_buf, stage1, recv1,
    agg_buf, aggcol, grad_buf, grad_all, out_stage, stage2, gbuf, stage3, recv3,
    back_own, loc_buf, wstage, wrecv, wall,
    local_sem, s0, r0, sc, rc, s1, r1, so, ro, sa, ra, sg, rg, s2, r2, s3, r3, s4, r4, s5, r5,
):
    rows, cols, reps = lax.axis_size("row"), lax.axis_size("col"), lax.axis_size("rep")
    r, c, p = lax.axis_index("row"), lax.axis_index("col"), lax.axis_index("rep")
    sub, width = feat_ref.shape
    piece = sub // reps
    row_tiles = sub * cols // TILE
    col_tiles = sub * rows // TILE
    edge_slots = edges_ref.shape[3]
    tile_slots = edges_ref.shape[2]

    def turn(at, by, size):
        return lax.rem(at + by, size)

    def back(at, by, size):
        return lax.rem(at + size - by, size)

    load = pltpu.make_async_copy(weight_hbm, weight_buf, local_sem.at[0])
    load.start()

    barrier = pltpu.get_barrier_semaphore()
    plane = [(dc, dp) for dc in range(cols) for dp in range(reps) if dc or dp]
    plane.sort(key=lambda at: -(min(at[0], cols - at[0]) * 4 + min(at[1], reps - at[1])))
    lane = [(dr, dc) for dr in range(rows) for dc in range(cols) if dr or dc]
    greet = [(0, dc, dp) for dc, dp in plane]
    greet += [(dr, dc, 0) for dr, dc in lane if dr and (fused or dc == 0)]
    for dr, dc, dp in greet:
        pl.semaphore_signal(
            barrier, inc=1, device_id=(turn(r, dr, rows), turn(c, dc, cols), turn(p, dp, reps)),
            device_id_type=MESH,
        )

    def push(src, dst, send, recv, to):
        copy = pltpu.make_async_remote_copy(
            src_ref=src, dst_ref=dst, send_sem=send, recv_sem=recv, device_id=to, device_id_type=MESH
        )
        copy.start()
        return copy

    slots = edges_ref[0, 0]
    live = slots >= 0
    targets = jnp.where(live, (slots >> 7) + 1, 0).astype(F32).astype(BF16)
    sources = jnp.where(live, (slots & 127) + 1, 0).astype(F32).astype(BF16)
    places = pos_ref[0]
    group = tsort.shape[2] // edge_slots
    for j in range(col_tiles):
        wanted = lax.broadcasted_iota(jnp.int32, (row_tiles, tile_slots), 0) * col_tiles + j
        pick = jnp.where(wanted == places, 1.0, 0.0).astype(BF16)
        g, k = j // group, j % group
        tsort[g, :, k * edge_slots:(k + 1) * edge_slots] = jnp.dot(
            pick, targets, preferred_element_type=F32
        )
        found = jnp.dot(pick, sources, preferred_element_type=F32)
        ssort[g, :, k * edge_slots:(k + 1) * edge_slots] = jnp.where(found > 0, found + k * 128.0, 0.0)

    pl.semaphore_wait(barrier, len(greet))
    feat_moves = [
        push(
            feat_ref, xbuf.at[pl.ds(pl.multiple_of(r * sub, sub), sub)], s0.at[dr], r0.at[dr],
            (turn(r, dr, rows), c, p),
        )
        for dr in range(1, rows)
    ]
    cot_moves = []
    for dp in range(1, reps):
        q = turn(p, dp, reps)
        cot_moves.append(
            push(
                cot_ref.at[pl.ds(pl.multiple_of(q * piece, piece), piece)], cot_buf.at[p],
                sc.at[dp], rc.at[dp], (r, c, q),
            )
        )
    cot_buf[p] = cot_ref[pl.ds(pl.multiple_of(p * piece, piece), piece)]
    xbuf[pl.ds(pl.multiple_of(r * sub, sub), sub)] = feat_ref[...]

    def build(i):
        at = pl.ds(start_of(i, TILE), TILE)
        for g in range(col_tiles // group):
            span = slice(g * group * TILE, (g + 1) * group * TILE)
            hot_t = one_hot(tsort[g, pl.ds(i, 1), :], TILE)
            hot_s = one_hot(ssort[g, pl.ds(i, 1), :], group * TILE)
            contract = (((1,), (1,)), ((), ()))
            adj[at, span] = lax.dot_general(hot_t, hot_s, contract, preferred_element_type=F32).astype(BF16)
            adj_t[span, at] = lax.dot_general(hot_s, hot_t, contract, preferred_element_type=F32).astype(BF16)

    repeat(row_tiles, build)

    for move in feat_moves:
        move.wait()

    def forward(i):
        at = pl.ds(start_of(i, TILE), TILE)
        stage1[at] = jnp.dot(adj[at], xbuf[...], preferred_element_type=F32).astype(BF16)

    repeat(row_tiles, forward)

    sum_moves = []
    for dc, dp in plane:
        to_c, to_p = turn(c, dc, cols), turn(p, dp, reps)
        first = pl.multiple_of((to_c * reps + to_p) * piece, piece)
        k = dc * reps + dp
        sum_moves.append(
            push(stage1.at[pl.ds(first, piece)], recv1.at[dc, p], s1.at[k], r1.at[k], (r, to_c, to_p))
        )
    recv1[0, p] = stage1[pl.ds(pl.multiple_of((c * reps + p) * piece, piece), piece)]

    ids0 = lax.broadcasted_iota(jnp.int32, (piece, sub), 0)
    ids1 = lax.broadcasted_iota(jnp.int32, (piece, sub), 1)
    degree = jnp.sum(
        jnp.where(ids1 == ids0 + p * piece, deg_ref[...].astype(F32), 0.0), axis=1, keepdims=True
    )
    inverse = 1.0 / degree
    load.wait()
    for move in cot_moves:
        move.wait()
    for move in sum_moves:
        move.wait()

    for q in range(reps):
        total = recv1[0, q].astype(F32)
        for dc in range(1, cols):
            total += recv1[dc, q].astype(F32)
        scaled_sum = (total * inverse).astype(BF16)
        agg_buf[q] = scaled_sum
    agg_moves = []
    for dp in range(1, reps):
        q = turn(p, dp, reps)
        agg_moves.append(push(agg_buf.at[q], aggcol.at[p], sa.at[dp], ra.at[dp], (r, c, q)))
    aggcol[p] = agg_buf[p]

    agg = jnp.concatenate([agg_buf[q] for q in range(reps)], axis=1)
    preact = jnp.dot(agg, weight_buf[...], preferred_element_type=F32)
    sigmoid = jax.nn.sigmoid(preact)
    output = (preact * sigmoid).astype(BF16)
    slope = sigmoid * (1.0 + preact * (1.0 - sigmoid))
    wide = cot_ref.shape[1]
    cot = jnp.concatenate([cot_buf[q] for q in range(reps)], axis=1)
    grad_pre = (cot.astype(F32) * slope).astype(BF16)
    grad_buf[...] = grad_pre
    grad_moves = []
    for dp in range(1, reps):
        q = turn(p, dp, reps)
        grad_moves.append(push(grad_buf, grad_all.at[p], sg.at[dp], rg.at[dp], (r, c, q)))
    grad_all[p] = grad_pre
    grad_agg = lax.dot_general(
        grad_pre, weight_buf[...], (((1,), (1,)), ((), ())), preferred_element_type=F32
    )
    scaled = (grad_agg * inverse).astype(BF16)
    for q in range(reps):
        stage2[q] = scaled[:, q * width:(q + 1) * width]
        out_stage[q] = output[:, q * wide:(q + 1) * wide]
    here = pl.ds(pl.multiple_of((c * reps + p) * piece, piece), piece)
    spread_moves = []
    for dc, dp in plane:
        to_c, to_p = turn(c, dc, cols), turn(p, dp, reps)
        k = dc * reps + dp
        spread_moves.append(push(stage2.at[to_p], gbuf.at[here], s2.at[k], r2.at[k], (r, to_c, to_p)))
    gbuf[here] = stage2[p]
    mine = pl.ds(pl.multiple_of(p * piece, piece), piece)
    out_moves = []
    for dp in range(1, reps):
        q = turn(p, dp, reps)
        out_moves.append(push(out_stage.at[q], out_ref.at[mine], so.at[dp], ro.at[dp], (r, c, q)))
    out_ref[mine] = out_stage[p]

    for move in agg_moves:
        move.wait()
    for move in grad_moves:
        move.wait()
    agg_cols = aggcol[...].reshape(sub, width)
    grad_rows = grad_all[...].reshape(sub, reps * wide)
    local = lax.dot_general(agg_cols, grad_rows, (((0,), (0,)), ((), ())), preferred_element_type=F32)
    if fused:
        part = width // (rows * cols)
        loc_buf[...] = local
        wstage[...] = local.astype(BF16)
        w_moves = []
        for dr, dc in lane:
            to_r, to_c = turn(r, dr, rows), turn(c, dc, cols)
            k = dr * cols + dc
            first = pl.multiple_of((to_r * cols + to_c) * part, part)
            w_moves.append(push(wstage.at[pl.ds(first, part)], wrecv.at[k], s4.at[k], r4.at[k], (to_r, to_c, p)))
    else:
        gw_ref[...] = local

    for move in spread_moves:
        move.wait()
    back_all = jnp.dot(adj_t[...], gbuf[...], preferred_element_type=F32)
    stage3[...] = back_all.astype(BF16)
    back_own[...] = back_all
    back_moves = []
    for dr in range(1, rows):
        to_r = turn(r, dr, rows)
        src = stage3.at[pl.ds(pl.multiple_of(to_r * sub, sub), sub)]
        back_moves.append(push(src, recv3.at[dr], s3.at[dr], r3.at[dr], (to_r, c, p)))

    if fused:
        own = pl.ds(pl.multiple_of((r * cols + c) * part, part), part)
        for move in w_moves:
            move.wait()
        total = loc_buf[own]
        for dr, dc in lane:
            total += wrecv[dr * cols + dc].astype(F32)
        wall[own] = total.astype(BF16)
        all_moves = []
        for dr, dc in lane:
            to_r, to_c = turn(r, dr, rows), turn(c, dc, cols)
            k = dr * cols + dc
            all_moves.append(push(wall.at[own], wall.at[own], s5.at[k], r5.at[k], (to_r, to_c, p)))

    for move in back_moves:
        move.wait()
    total = back_own[pl.ds(pl.multiple_of(r * sub, sub), sub)]
    for dr in range(1, rows):
        total += recv3[dr].astype(F32)
    gf_ref[...] = total.astype(BF16)
    for move in out_moves:
        move.wait()
    if fused:
        for move in all_moves:
            move.wait()
        gw_ref[...] = wall[...].astype(F32)


def body(features, weight, tile_pos, edges, degree, cotangent):
    rows, cols, reps = lax.axis_size("row"), lax.axis_size("col"), lax.axis_size("rep")
    sub, width = features.shape
    wide = cotangent.shape[1]
    piece = sub // reps
    f_in, f_out = weight.shape
    targets, sources = sub * cols, sub * rows
    row_tiles, col_tiles = targets // TILE, sources // TILE
    group = math.gcd(col_tiles, 4)
    fused = width % (rows * cols * 16) == 0
    part = width // (rows * cols) if fused else 16
    lanes = rows * cols if fused else 1
    dma = pltpu.SemaphoreType.DMA
    vmem = pl.BlockSpec(memory_space=pltpu.VMEM)
    scratch = [
        pltpu.VMEM((f_in, f_out), BF16),
        pltpu.VMEM((col_tiles // group, row_tiles, group * edges.shape[3]), F32),
        pltpu.VMEM((col_tiles // group, row_tiles, group * edges.shape[3]), F32),
        pltpu.VMEM((targets, sources), BF16),
        pltpu.VMEM((sources, targets), BF16),
        pltpu.VMEM((sources, width), BF16),
        pltpu.VMEM((reps, piece, wide), BF16),
        pltpu.VMEM((targets, width), BF16),
        pltpu.VMEM((cols, reps, piece, width), BF16),
        pltpu.VMEM((reps, piece, width), BF16),
        pltpu.VMEM((reps, piece, width), BF16),
        pltpu.VMEM((piece, f_out), BF16),
        pltpu.VMEM((reps, piece, f_out), BF16),
        pltpu.VMEM((reps, piece, wide), BF16),
        pltpu.VMEM((reps, piece, width), BF16),
        pltpu.VMEM((targets, width), BF16),
        pltpu.VMEM((sources, width), BF16),
        pltpu.VMEM((rows, sub, width), BF16),
        pltpu.VMEM((sources, width), F32),
        pltpu.VMEM((width, f_out), F32),
        pltpu.VMEM((width, f_out), BF16),
        pltpu.VMEM((lanes, part, f_out), BF16),
        pltpu.VMEM((width, f_out), BF16),
        dma((1,)),
    ]
    for count in (rows, reps, cols * reps, reps, reps, reps, cols * reps, rows, lanes, lanes):
        scratch += [dma((count,)), dma((count,))]
    output, grad_weight, grad_features = pl.pallas_call(
        functools.partial(kernel, fused),
        out_shape=(
            jax.ShapeDtypeStruct((sub, wide), BF16),
            jax.ShapeDtypeStruct((width, f_out), F32),
            jax.ShapeDtypeStruct((sub, width), BF16),
        ),
        in_specs=[vmem, pl.BlockSpec(memory_space=pl.ANY)] + [vmem] * 4,
        out_specs=(vmem, vmem, vmem),
        scratch_shapes=scratch,
        compiler_params=pltpu.CompilerParams(
            collective_id=0, has_side_effects=True, vmem_limit_bytes=52 * 1024 * 1024
        ),
    )(features, weight, tile_pos, edges, degree.reshape(1, sub), cotangent)
    if not fused:
        grad_weight = lax.psum(grad_weight, ("row", "col"))
    return output, grad_weight, grad_features


def solution(mesh):
    placed = (
        P(("col", "row"), "rep"),
        P(),
        P("row", "col", None),
        P("row", "col", None, None),
        P(("row", "col")),
        P(("row", "col"), "rep"),
    )
    return jax.shard_map(
        body,
        mesh=mesh,
        in_specs=placed,
        out_specs=(P(("row", "col"), "rep"), P("rep", None), P(("col", "row"), "rep")),
        check_vma=False,
    )
```

time: 214 us -> 42.3 us (0.20)
  waiting for transfers between devices: 106 us -> 0 us
  other arithmetic: 51.6 us -> 0 us
  Pallas kernels: 0 us -> 35.2 us
  blocking collectives: 32.2 us -> 0 us
  between operations: 13.9 us -> 0.66 us
  matrix products: 7.16 us -> 0 us
  local copies, waits for them, and re-layouts: 3.19 us -> 6.07 us
    psum x1 -> x0, waiting for transfers between devices: 73.4 us -> none  [body(): grad_weight = lax.psum(local_weight, ('row', 'col'))]
    scatter-add x2 -> x0, other arithmetic: 46.8 us -> none  [step(): return (totals.at[node_rows].add(flat, mode='drop'), None)]
    pallas_call x0 -> x1, Pallas kernels: none -> 35.2 us  [body(): pl.pallas_call(functools.partial(kernel, fused), out_shape=(jax.ShapeDtyp...]
    reduce_scatter x2 -> x0, waiting for transfers between devices: 32.4 us -> none  [the longest x1 23.4 us: body(): lax.psum_scatter(partial_value, 'col', scatter_dimension=0, tiled=True)]
    all_gather x4 -> x0, blocking collectives: 32.2 us -> none  [the longest x1 14.4 us: body(): target_rows = lax.all_gather(scaled, 'col', axis=0, tiled=True)]
    dot_general x6 -> x0, matrix products: 7.16 us -> none  [the longest x1 1.86 us: step(): jnp.einsum('gab,gaf->gbf', tiles, picked, preferred_element_type=jnp.floa...]
    unnamed x7 -> x15, local copies, waits for them, and re-layouts: 1.69 us -> 6.07 us
    convert_element_type x2 -> x0, other arithmetic: 2.54 us -> none  [the longest x1 1.54 us: body(): grad_features = back_total.astype(jnp.bfloat16)]
  transfers between devices with their start and end apart: 3 -> 0, of which waited for: 3 -> 0; matrix products, arithmetic and copies ran while one was open for 1% -> 0% of each run, Pallas kernels for 0% -> 0%
where the time goes in v1:
time: 42.3 us; the launch traced here: 42 us
  Pallas kernels  35.2 us (83%)
  local copies, waits for them, and re-layouts  6.07 us (14%)
  between operations  0.66 us (2%)
    pallas_call x1, Pallas kernels, body(): pl.pallas_call(functools.partial(kernel, fused), out_shape=(jax.ShapeDtyp...  35.2 us
    unnamed x15, local copies, waits for them, and re-layouts  6.07 us

profile of v1, /device:TPU:0, one launch (start us, length us, event | category | flops | bytes accessed | tf_op | source)
XLA Modules:
  0.0 42.0 jit_solution(14080779385425275785)
XLA Ops:
  0.6 0.0 copy-start.4
  0.6 0.0 copy-start.5
  0.7 0.7 %copy-done.4 = s32[256]{0:T(256)S(1)} copy-done((s32[256]{0:T(256)S(1)}, s32[256]{0:T(256)}, u32[]{:S(2)}) %copy-start.4) | copy-done | bytes 1048
  1.3 0.0 copy-done.5
  1.3 0.0 copy-start
  1.3 1.0 %copy-done = bf16[512,512]{1,0:T(8,128)(2,1)S(1)} copy-done((bf16[512,512]{1,0:T(8,128)(2,1)S(1)}, bf16[512,512]{1,0:T(8,128)(2,1)}, u32[]{:S(2)}) %copy-start) | copy-done | bytes 524312
  2.4 0.0 copy-start.1
  2.4 0.8 %copy-done.1 = bf16[256,128]{1,0:T(8,128)(2,1)S(1)} copy-done((bf16[256,128]{1,0:T(8,128)(2,1)S(1)}, bf16[256,128]{1,0:T(8,128)(2,1)}, u32[]{:S(2)}) %copy-start.1) | copy-done | bytes 65560
  3.2 0.0 copy-start.2
  3.2 0.8 %copy-done.2 = bf16[256,128]{1,0:T(8,128)(2,1)S(1)} copy-done((bf16[256,128]{1,0:T(8,128)(2,1)S(1)}, bf16[256,128]{1,0:T(8,128)(2,1)}, u32[]{:S(2)}) %copy-start.2) | copy-done | bytes 65560
  4.0 0.0 copy-start.3
  4.0 0.7 %copy-done.3 = s32[1,1,32,64]{3,2,1,0:T(8,128)S(1)} copy-done((s32[1,1,32,64]{3,2,1,0:T(8,128)S(1)}, s32[1,1,32,64]{3,2,1,0:T(8,128)}, u32[]{:S(2)}) %copy-start.3) | copy-done | bytes 8216
  4.8 35.2 %shard_map.85 = (bf16[256,128]{1,0:T(8,128)(2,1)S(1)}, f32[128,512]{1,0:T(8,128)S(1)}, bf16[256,128]{1,0:T(8,128)(2,1)S(1)}) custom-call(bf16[256,128]{1,0:T(8,128)(2,1)S(1)} %copy-done.1, bf16[512,512]{1,0:T(8,128)(2,1)S(1)} %copy-done, s32[1,1,32]{2,1,0:T(1,128)S(1)} %copy-done.5, s32[1,1,32,64]{3,2,1,0:T(8,128)S(1)} %copy-done.3, s32[1,256]{1,0:T(1,128)S(1)} %bitcast.1, ...), custom_call_target="tpu_custom_call" | custom-call | tf_op jit(solution)/shard_map/pallas_call | solution.py:307
  40.0 0.6 %copy.12 = bf16[256,128]{1,0:T(8,128)(2,1)} copy(bf16[256,128]{1,0:T(8,128)(2,1)S(1)} %get-tuple-element.6) | data formatting | bytes 131072
  40.6 0.7 %copy.13 = f32[128,512]{1,0:T(8,128)} copy(f32[128,512]{1,0:T(8,128)S(1)} %get-tuple-element.7) | data formatting | bytes 524288
  41.3 0.6 %copy.14 = bf16[256,128]{1,0:T(8,128)(2,1)} copy(bf16[256,128]{1,0:T(8,128)(2,1)S(1)} %get-tuple-element.8) | data formatting | bytes 131072
Async XLA Ops:
  0.6 0.7 %copy-start.4 = (s32[256]{0:T(256)S(1)}, s32[256]{0:T(256)}, u32[]{:S(2)}) copy-start(s32[256]{0:T(256)} %param.10) | copy-start | bytes 3076
  0.6 0.7 %copy-start.5 = (s32[1,1,32]{2,1,0:T(1,128)S(1)}, s32[1,1,32]{2,1,0:T(1,128)}, u32[]{:S(2)}) copy-start(s32[1,1,32]{2,1,0:T(1,128)} %pos_ref.1) | copy-start | bytes 388
  1.3 1.0 %copy-start = (bf16[512,512]{1,0:T(8,128)(2,1)S(1)}, bf16[512,512]{1,0:T(8,128)(2,1)}, u32[]{:S(2)}) copy-start(bf16[512,512]{1,0:T(8,128)(2,1)} %weight_hbm.1) | copy-start | bytes 1572868
  2.4 0.8 %copy-start.1 = (bf16[256,128]{1,0:T(8,128)(2,1)S(1)}, bf16[256,128]{1,0:T(8,128)(2,1)}, u32[]{:S(2)}) copy-start(bf16[256,128]{1,0:T(8,128)(2,1)} %feat_ref.1) | copy-start | bytes 196612
  3.2 0.8 %copy-start.2 = (bf16[256,128]{1,0:T(8,128)(2,1)S(1)}, bf16[256,128]{1,0:T(8,128)(2,1)}, u32[]{:S(2)}) copy-start(bf16[256,128]{1,0:T(8,128)(2,1)} %cot_ref.1) | copy-start | bytes 196612
  4.0 0.7 %copy-start.3 = (s32[1,1,32,64]{3,2,1,0:T(8,128)S(1)}, s32[1,1,32,64]{3,2,1,0:T(8,128)}, u32[]{:S(2)}) copy-start(s32[1,1,32,64]{3,2,1,0:T(8,128)} %edges_ref.1) | copy-start | bytes 24580

commit v2 on v1

--- a/solution.py
+++ b/solution.py
@@ -33,12 +33,12 @@
 
 def kernel(
     fused,
-    feat_ref, weight_hbm, pos_ref, edges_ref, deg_ref, cot_ref,
+    feat_hbm, weight_hbm, pos_hbm, edges_hbm, deg_hbm, cot_hbm,
     out_ref, gw_ref, gf_ref,
-    weight_buf, tsort, ssort, adj, adj_t, xbuf, cot_buf, stage1, recv1,
+    feat_ref, weight_buf, weight_t, pos_ref, edges_ref, deg_ref, cot_ref, tsort, ssort, adj, adj_t, xbuf, cot_buf, stage1, recv1,
     agg_buf, aggcol, grad_buf, grad_all, out_stage, stage2, gbuf, stage3, recv3,
-    back_own, loc_buf, wstage, wrecv, wall,
-    local_sem, s0, r0, sc, rc, s1, r1, so, ro, sa, ra, sg, rg, s2, r2, s3, r3, s4, r4, s5, r5,
+    back_own, loc_buf, wstage, wrow, hsum, hstage, wrecv, wall,
+    local_sem, s0, r0, sc, rc, s1, r1, so, ro, sa, ra, sg, rg, s2, r2, s3, r3, s4, r4, s5, r5, s6, r6,
 ):
     rows, cols, reps = lax.axis_size("row"), lax.axis_size("col"), lax.axis_size("rep")
     r, c, p = lax.axis_index("row"), lax.axis_index("col"), lax.axis_index("rep")
@@ -55,8 +55,13 @@
     def back(at, by, size):
         return lax.rem(at + size - by, size)
 
-    load = pltpu.make_async_copy(weight_hbm, weight_buf, local_sem.at[0])
-    load.start()
+    pairs = (
+        (pos_hbm, pos_ref), (edges_hbm, edges_ref), (feat_hbm, feat_ref),
+        (cot_hbm, cot_ref), (deg_hbm, deg_ref), (weight_hbm, weight_buf),
+    )
+    loads = [pltpu.make_async_copy(src, dst, local_sem.at[k]) for k, (src, dst) in enumerate(pairs)]
+    for load in loads:
+        load.start()
 
     barrier = pltpu.get_barrier_semaphore()
     plane = [(dc, dp) for dc in range(cols) for dp in range(reps) if dc or dp]
@@ -77,6 +82,26 @@
         copy.start()
         return copy
 
+    pl.semaphore_wait(barrier, len(greet))
+    feat_moves = [
+        push(
+            feat_hbm, xbuf.at[pl.ds(pl.multiple_of(r * sub, sub), sub)], s0.at[dr], r0.at[dr],
+            (turn(r, dr, rows), c, p),
+        )
+        for dr in range(1, rows)
+    ]
+    cot_moves = []
+    for dp in range(1, reps):
+        q = turn(p, dp, reps)
+        cot_moves.append(
+            push(
+                cot_hbm.at[pl.ds(pl.multiple_of(q * piece, piece), piece)], cot_buf.at[p],
+                sc.at[dp], rc.at[dp], (r, c, q),
+            )
+        )
+
+    loads[0].wait()
+    loads[1].wait()
     slots = edges_ref[0, 0]
     live = slots >= 0
     targets = jnp.where(live, (slots >> 7) + 1, 0).astype(F32).astype(BF16)
@@ -93,23 +118,8 @@
         found = jnp.dot(pick, sources, preferred_element_type=F32)
         ssort[g, :, k * edge_slots:(k + 1) * edge_slots] = jnp.where(found > 0, found + k * 128.0, 0.0)
 
-    pl.semaphore_wait(barrier, len(greet))
-    feat_moves = [
-        push(
-            feat_ref, xbuf.at[pl.ds(pl.multiple_of(r * sub, sub), sub)], s0.at[dr], r0.at[dr],
-            (turn(r, dr, rows), c, p),
-        )
-        for dr in range(1, rows)
-    ]
-    cot_moves = []
-    for dp in range(1, reps):
-        q = turn(p, dp, reps)
-        cot_moves.append(
-            push(
-                cot_ref.at[pl.ds(pl.multiple_of(q * piece, piece), piece)], cot_buf.at[p],
-                sc.at[dp], rc.at[dp], (r, c, q),
-            )
-        )
+    loads[2].wait()
+    loads[3].wait()
     cot_buf[p] = cot_ref[pl.ds(pl.multiple_of(p * piece, piece), piece)]
     xbuf[pl.ds(pl.multiple_of(r * sub, sub), sub)] = feat_ref[...]
 
@@ -144,15 +154,17 @@
         )
     recv1[0, p] = stage1[pl.ds(pl.multiple_of((c * reps + p) * piece, piece), piece)]
 
+    loads[4].wait()
     ids0 = lax.broadcasted_iota(jnp.int32, (piece, sub), 0)
     ids1 = lax.broadcasted_iota(jnp.int32, (piece, sub), 1)
     degree = jnp.sum(
         jnp.where(ids1 == ids0 + p * piece, deg_ref[...].astype(F32), 0.0), axis=1, keepdims=True
     )
     inverse = 1.0 / degree
-    load.wait()
+    loads[5].wait()
     for move in cot_moves:
         move.wait()
+    weight_t[...] = weight_buf[...].T
     for move in sum_moves:
         move.wait()
 
@@ -178,50 +190,69 @@
     grad_pre = (cot.astype(F32) * slope).astype(BF16)
     grad_buf[...] = grad_pre
     grad_moves = []
-    for dp in range(1, reps):
-        q = turn(p, dp, reps)
-        grad_moves.append(push(grad_buf, grad_all.at[p], sg.at[dp], rg.at[dp], (r, c, q)))
+    relay = reps == 4
+    beside, across = p + 1 - 2 * lax.rem(p, 2), lax.rem(p + 2, 4)
+    if relay:
+        far_move = push(grad_buf, grad_all.at[p], sg.at[2], rg.at[2], (r, c, across))
+        grad_moves.append(push(grad_buf, grad_all.at[p], sg.at[1], rg.at[1], (r, c, beside)))
+    else:
+        for dp in range(1, reps):
+            q = turn(p, dp, reps)
+            grad_moves.append(push(grad_buf, grad_all.at[p], sg.at[dp], rg.at[dp], (r, c, q)))
     grad_all[p] = grad_pre
-    grad_agg = lax.dot_general(
-        grad_pre, weight_buf[...], (((1,), (1,)), ((), ())), preferred_element_type=F32
-    )
+    grad_agg = jnp.dot(grad_pre, weight_t[...], preferred_element_type=F32)
     scaled = (grad_agg * inverse).astype(BF16)
     for q in range(reps):
         stage2[q] = scaled[:, q * width:(q + 1) * width]
         out_stage[q] = output[:, q * wide:(q + 1) * wide]
     here = pl.ds(pl.multiple_of((c * reps + p) * piece, piece), piece)
+    gbuf[here] = stage2[p]
+    mine = pl.ds(pl.multiple_of(p * piece, piece), piece)
+    if relay:
+        far_move.wait()
+        grad_moves.append(push(grad_all.at[across], grad_all.at[across], sg.at[3], rg.at[3], (r, c, beside)))
     spread_moves = []
     for dc, dp in plane:
         to_c, to_p = turn(c, dc, cols), turn(p, dp, reps)
         k = dc * reps + dp
         spread_moves.append(push(stage2.at[to_p], gbuf.at[here], s2.at[k], r2.at[k], (r, to_c, to_p)))
-    gbuf[here] = stage2[p]
-    mine = pl.ds(pl.multiple_of(p * piece, piece), piece)
+    for move in agg_moves:
+        move.wait()
+    for move in grad_moves:
+        move.wait()
+    agg_cols = aggcol[...].reshape(sub, width)
+    grad_rows = grad_all[...].reshape(sub, reps * wide)
+    local = lax.dot_general(agg_cols, grad_rows, (((0,), (0,)), ((), ())), preferred_element_type=F32)
+    if fused:
+        part = width // (rows * cols)
+        half = width // rows
+        loc_buf[...] = local
+        wstage[...] = local.astype(BF16)
+        row_moves = []
+        for dr in range(1, rows):
+            to_r = turn(r, dr, rows)
+            first = pl.multiple_of(to_r * half, half)
+            row_moves.append(push(wstage.at[pl.ds(first, half)], wrow.at[dr], s6.at[dr], r6.at[dr], (to_r, c, p)))
+        for move in row_moves:
+            move.wait()
+        total = loc_buf[pl.ds(pl.multiple_of(r * half, half), half)]
+        for dr in range(1, rows):
+            total += wrow[dr].astype(F32)
+        hsum[...] = total
+        hstage[...] = total.astype(BF16)
+        w_moves = []
+        for dc in range(1, cols):
+            to_c = turn(c, dc, cols)
+            first = pl.multiple_of(to_c * part, part)
+            w_moves.append(push(hstage.at[pl.ds(first, part)], wrecv.at[dc], s4.at[dc], r4.at[dc], (r, to_c, p)))
+    else:
+        gw_ref[...] = local
+
     out_moves = []
     for dp in range(1, reps):
         q = turn(p, dp, reps)
         out_moves.append(push(out_stage.at[q], out_ref.at[mine], so.at[dp], ro.at[dp], (r, c, q)))
     out_ref[mine] = out_stage[p]
-
-    for move in agg_moves:
-        move.wait()
-    for move in grad_moves:
-        move.wait()
-    agg_cols = aggcol[...].reshape(sub, width)
-    grad_rows = grad_all[...].reshape(sub, reps * wide)
-    local = lax.dot_general(agg_cols, grad_rows, (((0,), (0,)), ((), ())), preferred_element_type=F32)
-    if fused:
-        part = width // (rows * cols)
-        loc_buf[...] = local
-        wstage[...] = local.astype(BF16)
-        w_moves = []
-        for dr, dc in lane:
-            to_r, to_c = turn(r, dr, rows), turn(c, dc, cols)
-            k = dr * cols + dc
-            first = pl.multiple_of((to_r * cols + to_c) * part, part)
-            w_moves.append(push(wstage.at[pl.ds(first, part)], wrecv.at[k], s4.at[k], r4.at[k], (to_r, to_c, p)))
-    else:
-        gw_ref[...] = local
 
     for move in spread_moves:
         move.wait()
@@ -238,9 +269,9 @@
         own = pl.ds(pl.multiple_of((r * cols + c) * part, part), part)
         for move in w_moves:
             move.wait()
-        total = loc_buf[own]
-        for dr, dc in lane:
-            total += wrecv[dr * cols + dc].astype(F32)
+        total = hsum[pl.ds(pl.multiple_of(c * part, part), part)]
+        for dc in range(1, cols):
+            total += wrecv[dc].astype(F32)
         wall[own] = total.astype(BF16)
         all_moves = []
         for dr, dc in lane:
@@ -260,6 +291,15 @@
         for move in all_moves:
             move.wait()
         gw_ref[...] = wall[...].astype(F32)
+
+
+def store(*refs):
+    sems = refs[-1]
+    moves = [pltpu.make_async_copy(refs[k], refs[k + 3], sems.at[k]) for k in range(3)]
+    for move in moves:
+        move.start()
+    for move in moves:
+        move.wait()
 
 
 def body(features, weight, tile_pos, edges, degree, cotangent):
@@ -274,10 +314,19 @@
     fused = width % (rows * cols * 16) == 0
     part = width // (rows * cols) if fused else 16
     lanes = rows * cols if fused else 1
+    half = part * cols if fused else 16
     dma = pltpu.SemaphoreType.DMA
+    grant = 61 * 1024 * 1024
     vmem = pl.BlockSpec(memory_space=pltpu.VMEM)
+    hbm = pl.BlockSpec(memory_space=pltpu.HBM)
     scratch = [
+        pltpu.VMEM(features.shape, BF16),
         pltpu.VMEM((f_in, f_out), BF16),
+        pltpu.VMEM((f_out, f_in), BF16),
+        pltpu.VMEM(tile_pos.shape, jnp.int32),
+        pltpu.VMEM(edges.shape, jnp.int32),
+        pltpu.VMEM((1, sub), jnp.int32),
+        pltpu.VMEM(cotangent.shape, BF16),
         pltpu.VMEM((col_tiles // group, row_tiles, group * edges.shape[3]), F32),
         pltpu.VMEM((col_tiles // group, row_tiles, group * edges.shape[3]), F32),
         pltpu.VMEM((targets, sources), BF16),
@@ -298,11 +347,14 @@
         pltpu.VMEM((sources, width), F32),
         pltpu.VMEM((width, f_out), F32),
         pltpu.VMEM((width, f_out), BF16),
-        pltpu.VMEM((lanes, part, f_out), BF16),
+        pltpu.VMEM((rows if fused else 1, half, f_out), BF16),
+        pltpu.VMEM((half, f_out), F32),
+        pltpu.VMEM((half, f_out), BF16),
+        pltpu.VMEM((cols, part, f_out), BF16),
         pltpu.VMEM((width, f_out), BF16),
-        dma((1,)),
+        dma((6,)),
     ]
-    for count in (rows, reps, cols * reps, reps, reps, reps, cols * reps, rows, lanes, lanes):
+    for count in (rows, reps, cols * reps, reps, reps, reps, cols * reps, rows, cols, lanes, rows):
         scratch += [dma((count,)), dma((count,))]
     output, grad_weight, grad_features = pl.pallas_call(
         functools.partial(kernel, fused),
@@ -311,16 +363,24 @@
             jax.ShapeDtypeStruct((width, f_out), F32),
             jax.ShapeDtypeStruct((sub, width), BF16),
         ),
-        in_specs=[vmem, pl.BlockSpec(memory_space=pl.ANY)] + [vmem] * 4,
-        out_specs=(vmem, vmem, vmem),
+        in_specs=[hbm] * 6,
+        out_specs=(vmem,) * 3,
         scratch_shapes=scratch,
         compiler_params=pltpu.CompilerParams(
-            collective_id=0, has_side_effects=True, vmem_limit_bytes=52 * 1024 * 1024
+            collective_id=0, has_side_effects=True, vmem_limit_bytes=grant
         ),
     )(features, weight, tile_pos, edges, degree.reshape(1, sub), cotangent)
     if not fused:
         grad_weight = lax.psum(grad_weight, ("row", "col"))
-    return output, grad_weight, grad_features
+    results = (output, grad_weight, grad_features)
+    return pl.pallas_call(
+        store,
+        out_shape=tuple(jax.ShapeDtypeStruct(result.shape, result.dtype) for result in results),
+        in_specs=[vmem] * 3,
+        out_specs=(hbm,) * 3,
+        scratch_shapes=[dma((3,))],
+        compiler_params=pltpu.CompilerParams(vmem_limit_bytes=grant),
+    )(*results)
 
 
 def solution(mesh):

time: 42.3 us -> 38.4 us (0.908)
  local copies, waits for them, and re-layouts: 6.07 us -> 0 us
  Pallas kernels: 35.2 us -> 37.6 us
    unnamed x15 -> x0, local copies, waits for them, and re-layouts: 6.07 us -> none
    pallas_call x0 -> x1, Pallas kernels: none -> 1.71 us  [body(): pl.pallas_call(store, out_shape=tuple((jax.ShapeDtypeStruct(result.shape,...]
    pallas_call x1, Pallas kernels: 35.2 us -> 35.9 us  [body(): pl.pallas_call(functools.partial(kernel, fused), out_shape=(jax.ShapeDtyp...]
where the time goes in v2:
time: 38.4 us; the launch traced here: 38.2 us
  Pallas kernels  37.6 us (98%)
  between operations  0.64 us (2%)
    pallas_call x1, Pallas kernels, body(): pl.pallas_call(functools.partial(kernel, fused), out_shape=(jax.ShapeDtyp...  35.9 us
    pallas_call x1, Pallas kernels, body(): pl.pallas_call(store, out_shape=tuple((jax.ShapeDtypeStruct(result.shape,...  1.71 us

profile of v2, /device:TPU:0, one launch (start us, length us, event | category | flops | bytes accessed | tf_op | source)
XLA Modules:
  0.0 38.2 jit_solution(17882724361170974418)
XLA Ops:
  0.6 35.9 %shard_map.85 = (bf16[256,128]{1,0:T(8,128)(2,1)}, f32[128,512]{1,0:T(8,128)}, bf16[256,128]{1,0:T(8,128)(2,1)}) custom-call(bf16[256,128]{1,0:T(8,128)(2,1)} %feat_hbm.1, bf16[512,512]{1,0:T(8,128)(2,1)} %weight_hbm.1, s32[1,1,32]{2,1,0:T(1,128)} %pos_hbm.1, s32[1,1,32,64]{3,2,1,0:T(8,128)} %edges_hbm.1, s32[1,256]{1,0:T(1,128)} %bitcast.1, ...), custom_call_target="tpu_custom_call" | custom-call | tf_op jit(solution)/shard_map/pallas_call | solution.py:359
  36.5 1.7 %shard_map.86 = (bf16[256,128]{1,0:T(8,128)(2,1)}, f32[128,512]{1,0:T(8,128)}, bf16[256,128]{1,0:T(8,128)(2,1)}) custom-call(bf16[256,128]{1,0:T(8,128)(2,1)} %get-tuple-element.6.refs_0_, f32[128,512]{1,0:T(8,128)} %get-tuple-element.7.refs_1_, bf16[256,128]{1,0:T(8,128)(2,1)} %get-tuple-element.8.refs_2_), custom_call_target="tpu_custom_call" | custom-call | tf_op jit(solution)/shard_map/pallas_call | solution.py:376
